TPU v7x, 256 devices: a whole 4x4x8 slice. The times are simulated.
256 devices in a mesh: grp: 16 (over z_lo, x, core), tp: 16 (over z_hi, y).
Axes of the slice: x: 4, y: 4, z: 8 (z_hi: 4, z_lo: 2; z = z_hi * 2 + z_lo), core: 2. Of those that a mesh axis runs over, the one named last changes fastest.
Arguments:
- image: bfloat16 [32768, 1280], P(('grp', 'tp')), may hold values from -6 to 6
- text: bfloat16 [4096, 8192], P(('grp', 'tp')), may hold values from -6 to 6
- ln_gain: float32 [1280], replicated, may hold values from 0.5 to 1.5
- ln_bias: float32 [1280], replicated, may hold values from -3 to 3
- w_up: bfloat16 [1280, 5120], P(None, 'tp'), may hold values from -0.15625 to 0.15625
- b_up: float32 [5120], P('tp'), may hold values from -3 to 3
- w_down: bfloat16 [5120, 1280], P('tp'), may hold values from -0.078125 to 0.078125
- b_down: float32 [1280], replicated, may hold values from -3 to 3
- tile_count: int32 [32], P('grp'), may hold values from 1 to 4, as said below
- assign: int32 [32], P('grp'), may hold values from 0 to 1
- w_key: bfloat16 [1280, 2048], P(None, 'tp'), may hold values from -0.15625 to 0.15625
- w_value: bfloat16 [1280, 2048], P(None, 'tp'), may hold values from -0.15625 to 0.15625
- in_gain: float32 [8192], replicated, may hold values from 0.4 to 2.5
- w_query: bfloat16 [8192, 4096], P(None, 'tp'), may hold values from -0.0625 to 0.0625
- q_gain: float32 [128], replicated, may hold values from 0.25 to 1.75
- k_gain: float32 [128], replicated, may hold values from 0.4 to 2.5
- w_out: bfloat16 [4096, 8192], P('tp'), may hold values from -0.09375 to 0.09375
- attn_gate: float32 [1], replicated, may hold values from 0.4 to 1.2
- amax_hist: float32 [16, 4], replicated, may hold values from 1.5 to 4.5
Outputs:
- mixed: bfloat16 [4096, 8192], P(('grp', 'tp'))
- image_features: bfloat16 [32768, 1280], P(('grp', 'tp'))
- amax_next: float32 [16, 4], replicated
Inputs may be any that keep to these rules, and one draw needn't show every extreme that they name: The first tile_count times 256 tokens of an image sample are valid.
All inputs are finite; a program needn't handle non-finite values.
Results may differ from a plain program's by a relative error of at most 0.018.
Values may be sent and summed in bfloat16 or wider, within the bound.
A program may use at most 64 MiB of HBM per device.

v0:
```python
import jax
import jax.numpy as jnp
from jax import lax
from jax.sharding import PartitionSpec as P

TILES = 4


def passed_along(value, axis, by):
    count = lax.axis_size(axis)
    return lax.ppermute(value, axis, [(i, (i + by) % count) for i in range(count)])


def layer_norm(values, gain, bias):
    centre = jnp.mean(values, axis=-1, keepdims=True)
    centred = values - centre
    spread = jnp.mean(centred * centred, axis=-1, keepdims=True)
    return centred * lax.rsqrt(spread + 1e-05) * gain + bias


def rms_norm(values, gain, small):
    return values * lax.rsqrt(jnp.mean(values * values, axis=-1, keepdims=True) + small) * gain


def local(
    image,
    text,
    ln_gain,
    ln_bias,
    w_up,
    b_up,
    w_down,
    b_down,
    tile_count,
    assign,
    w_key,
    w_value,
    in_gain,
    w_query,
    q_gain,
    k_gain,
    w_out,
    attn_gate,
    amax_hist,
):
    limits = jnp.max(amax_hist, axis=0)
    head_dim = k_gain.shape[0]
    image_f = image.astype(jnp.float32)
    normed = layer_norm(image_f, ln_gain, ln_bias)
    cur_input = jnp.max(jnp.abs(normed))
    cur_input = lax.pmax(cur_input, ("grp", "tp"))
    normed_c = jnp.clip(normed, -limits[0], limits[0]).astype(jnp.bfloat16)
    hidden = jax.nn.gelu(
        jnp.dot(
            lax.all_gather(normed_c, "tp", axis=0, tiled=True),
            w_up,
            preferred_element_type=jnp.float32,
        )
        + b_up,
        approximate=False,
    )
    cur_hidden = jnp.max(jnp.abs(hidden))
    cur_hidden = lax.pmax(cur_hidden, ("grp", "tp"))
    hidden_c = jnp.clip(hidden, -limits[1], limits[1]).astype(jnp.bfloat16)
    summed = lax.psum_scatter(
        jnp.dot(hidden_c, w_down, preferred_element_type=jnp.float32).astype(jnp.bfloat16),
        "tp",
        scatter_dimension=0,
        tiled=True,
    ).astype(jnp.float32)
    feature = image_f + summed + b_down
    cur_feature = jnp.max(jnp.abs(feature))
    cur_feature = lax.pmax(cur_feature, ("grp", "tp"))
    features = jnp.clip(feature, -limits[2], limits[2]).astype(jnp.bfloat16)
    moved, counts = passed_along((features, tile_count), "grp", 1)
    piece = lax.all_gather(moved, "tp", axis=0, tiled=True)
    projected = jnp.concatenate(
        [
            jnp.dot(piece, w_key, preferred_element_type=jnp.float32),
            jnp.dot(piece, w_value, preferred_element_type=jnp.float32),
        ],
        axis=1,
    )
    keys = rms_norm(projected[:, :head_dim], k_gain, 1e-06).astype(jnp.bfloat16)
    keys, values = (keys, projected[:, head_dim:].astype(jnp.bfloat16))
    img_samples = tile_count.shape[0]
    img_tokens = keys.shape[0] // img_samples
    keys = keys.reshape(img_samples, img_tokens, head_dim)
    values = values.reshape(img_samples, img_tokens, head_dim)
    text_f = text.astype(jnp.float32)
    tnormed = rms_norm(text_f, in_gain, 1e-05)
    cur_text = jnp.max(jnp.abs(tnormed))
    cur_text = lax.pmax(cur_text, ("grp", "tp"))
    tnormed_c = jnp.clip(tnormed, -limits[3], limits[3]).astype(jnp.bfloat16)
    query = jnp.dot(
        lax.all_gather(tnormed_c, "tp", axis=0, tiled=True),
        w_query,
        preferred_element_type=jnp.float32,
    )
    txt_samples = assign.shape[0]
    heads = query.shape[1] // head_dim
    query = rms_norm(query.reshape(query.shape[0], heads, head_dim), q_gain, 1e-06).astype(
        jnp.bfloat16
    )
    query = query.reshape(txt_samples, -1, heads, head_dim)
    key_sel = jnp.take(keys, assign, axis=0)
    value_sel = jnp.take(values, assign, axis=0)
    count_sel = jnp.take(counts, assign)
    scores = jnp.einsum(
        "sthd,skd->shtk", query, key_sel, preferred_element_type=jnp.float32
    ) * head_dim ** (-0.5)
    tile_tokens = img_tokens // TILES
    positions = lax.broadcasted_iota(jnp.int32, (txt_samples, img_tokens), 1)
    valid = (positions < (count_sel * tile_tokens)[:, None]).astype(jnp.float32)
    weights = jnp.exp(scores) * valid[:, None, None, :]
    weights = (weights / jnp.sum(weights, axis=-1, keepdims=True)).astype(jnp.bfloat16)
    attended = jnp.einsum(
        "shtk,skd->sthd", weights, value_sel, preferred_element_type=jnp.float32
    ).astype(jnp.bfloat16)
    attended = attended.reshape(-1, heads * head_dim)
    total = lax.psum_scatter(
        jnp.dot(attended, w_out, preferred_element_type=jnp.float32).astype(jnp.bfloat16),
        "tp",
        scatter_dimension=0,
        tiled=True,
    ).astype(jnp.float32)
    mixed = (text_f + jnp.tanh(attn_gate[0]) * total).astype(jnp.bfloat16)
    current = jnp.stack([cur_input, cur_hidden, cur_feature, cur_text])
    amax_next = jnp.concatenate([current[None, :], amax_hist[:-1]], axis=0)
    return (mixed, features, amax_next)


def solution(mesh):
    in_specs = (
        P(("grp", "tp"), None),
        P(("grp", "tp"), None),
        P(),
        P(),
        P(None, "tp"),
        P("tp"),
        P("tp", None),
        P(),
        P("grp"),
        P("grp"),
        P(None, "tp"),
        P(None, "tp"),
        P(),
        P(None, "tp"),
        P(),
        P(),
        P("tp", None),
        P(),
        P(),
    )
    out_specs = (P(("grp", "tp"), None), P(("grp", "tp"), None), P())
    return jax.shard_map(local, mesh=mesh, in_specs=in_specs, out_specs=out_specs, check_vma=False)
```

profile of v0, /device:TPU:40, one launch (start us, length us, event | category | flops | bytes accessed | tf_op | source)
XLA Modules:
  0.0 582.8 jit_solution(10193367264984461255)
XLA Ops:
  7.2 0.0 copy-start
  7.2 0.0 all-gather.4.cloned.1.call-start
  7.2 1.2 convert_reduce_fusion
  8.4 1.2 fusion.16
  9.6 0.8 reduce_max.45
  10.4 0.6 fusion.49
  11.7 2.7 fusion.22
  14.4 0.0 all-gather.4.cloned.1.call-update
  14.4 0.0 reduce-scatter.3.cloned.1.call-start
  15.1 89.6 %all-gather.4.cloned.1.call-done = bf16[2048,1280]{1,0:T(8,128)(2,1)} async-done(((bf16[128,1280]{1,0:T(8,128)(2,1)}), bf16[2048,1280]{1,0:T(8,128)(2,1)}) %all-gather.4.cloned.1.call-update) | async-done | bytes 5242896 | tf_op jit(solution)/shard_map/all_gather | solution.py:55
  104.6 10.2 %abs_reduce_fusion = (f32[]{:T(128)}, bf16[2048,320]{0,1:T(8,128)(2,1)S(1)}) fusion(f32[320]{0:T(512)} %param.26, bf16[2048,1280]{1,0:T(8,128)(2,1)} %all-gather.4.cloned.1.call-done, bf16[1280,320]{0,1:T(8,128)(2,1)} %param.25), kind=kOutput, calls=%fused_computation.9 | convolution fusion | flops 1722286080 | bytes 7374084 | tf_op jit(solution)/shard_map/dot_general | solution.py:54
  114.9 0.0 copy-done
  114.9 5.3 convolution_convert_fusion.1
  120.2 0.0 copy-start.14
  120.2 0.0 copy-start.12
  120.2 0.0 reduce-scatter.3.cloned.1.call-update
  120.2 0.0 all-gather.8.cloned.1.call-start
  121.0 0.1 copy-done.2
  121.1 0.2 fusion.25
  121.3 1.5 fusion.30
  122.8 0.0 all-gather.8.cloned.1.call-update
  122.9 0.0 all-gather.6.cloned.1.call-start
  123.5 94.3 %reduce-scatter.3.cloned.1.call-done = bf16[128,1280]{1,0:T(8,128)(2,1)} async-done(((bf16[2048,1280]{1,0:T(8,128)(2,1)}), bf16[128,1280]{1,0:T(8,128)(2,1)}) %reduce-scatter.3.cloned.1.call-update) | async-done | bytes 327696 | tf_op jit(solution)/shard_map/reduce_scatter | solution.py:65
  217.8 0.0 copy-done.9
  217.8 1.7 minimum_convert_fusion.2
  219.5 0.0 copy-start.4
  219.5 0.1 collective-permute-start
  219.6 8.6 %collective-permute-done = bf16[128,1280]{1,0:T(8,128)(2,1)S(1)} collective-permute-done((bf16[128,1280]{1,0:T(8,128)(2,1)S(1)}, bf16[128,1280]{1,0:T(8,128)(2,1)S(1)}, u32[]{:S(2)}, u32[]{:S(2)}) %collective-permute-start) | collective-permute-done | bytes 327712 | tf_op jit(solution)/shard_map/ppermute | solution.py:11
  228.2 0.7 copy-done.5
  228.9 0.0 all-gather.6.cloned.1.call-update
  228.9 0.0 reduce-scatter.5.cloned.1.call-start
  229.0 0.0 copy-done.14
  229.0 0.3 collective-permute-start.1
  229.3 0.0 copy-done.12
  229.3 5.0 collective-permute-done.1
  234.3 0.6 gather_fusion
  235.0 0.1 compare_convert_fusion
  235.0 62.6 %all-gather.8.cloned.1.call-done = bf16[256,8192]{1,0:T(8,128)(2,1)} async-done(((bf16[16,8192]{1,0:T(8,128)(2,1)}), bf16[256,8192]{1,0:T(8,128)(2,1)}) %all-gather.8.cloned.1.call-update) | async-done | bytes 4194320 | tf_op jit(solution)/shard_map/all_gather | solution.py:96
  297.6 5.2 bitcast_reduce_fusion.1
  302.8 0.0 copy-done.4
  302.8 0.1 reshape.106
  303.0 0.1 copy.25
  303.1 0.0 copy-start.11
  303.1 82.6 %all-gather.6.cloned.1.call-done = bf16[2048,1280]{1,0:T(8,128)(2,1)} async-done(((bf16[128,1280]{1,0:T(8,128)(2,1)}), bf16[2048,1280]{1,0:T(8,128)(2,1)}) %all-gather.6.cloned.1.call-update) | async-done | bytes 5242896 | tf_op jit(solution)/shard_map/all_gather | solution.py:76
  385.8 4.1 multiply_reduce_fusion
  389.9 0.3 multiply_convert_fusion
  390.3 0.6 gather_fusion.2
  390.9 0.0 copy-start.15
  390.9 4.1 convolution_convert_fusion.2
  395.0 0.6 gather_fusion.1
  395.7 0.7 bitcast_reduce_fusion
  396.4 0.8 fusion.12
  397.2 0.1 copy.28
  397.3 5.4 convolution_convert_fusion
  402.7 0.0 reduce-scatter.5.cloned.1.call-update
  403.5 0.2 copy-done.3
  403.7 0.0 copy-done.8
  403.7 0.9 fusion.23
  404.6 91.1 %reduce-scatter.5.cloned.1.call-done = bf16[16,8192]{1,0:T(8,128)(2,1)} async-done(((bf16[256,8192]{1,0:T(8,128)(2,1)}), bf16[16,8192]{1,0:T(8,128)(2,1)}) %reduce-scatter.5.cloned.1.call-update) | async-done | bytes 262160 | tf_op jit(solution)/shard_map/reduce_scatter | solution.py:121
  495.8 2.4 fusion.31
  498.2 74.7 %all-reduce = (f32[1]{0:T(128)}, f32[1]{0:T(128)}, f32[1]{0:T(128)}, f32[1]{0:T(128)}) all-reduce(f32[1]{0:T(128)} %bitcast.17, f32[1]{0:T(128)} %bitcast.16, f32[1]{0:T(128)} %bitcast.15, f32[1]{0:T(128)} %bitcast.14), channel_id=1, replica_groups=mesh['grp'=16,'tp'=16] {'grp','tp'}, use_global_device_ids=true, to_apply=%region_16.18 | all-reduce | flops 4 | bytes 32 | tf_op jit(solution)/shard_map/pmax | solution.py:93
  572.9 2.6 maximum_bitcast_fusion
  575.5 0.1 copy.29
  575.6 0.7 pad_maximum_fusion
  (25 shorter events, 0.1 us)
Async XLA Ops:
  7.2 107.7 %copy-start = (bf16[320,1280]{1,0:T(8,128)(2,1)S(1)}, bf16[320,1280]{1,0:T(8,128)(2,1)}, u32[]{:S(2)}) copy-start(bf16[320,1280]{1,0:T(8,128)(2,1)} %param.27) | copy-start | bytes 2457604
  7.2 97.4 %all-gather.4.cloned.1.call-start = ((), (), s32[]{:S(2)}) async-start(), calls=%async_computation.2 | async-start | bytes 5570560 | tf_op jit(solution)/shard_map/all_gather | solution.py:55
  14.4 203.4 %reduce-scatter.3.cloned.1.call-start = ((), (), s32[]{:S(2)}) async-start(), calls=%async_computation.3 | async-start | bytes 5570560 | tf_op jit(solution)/shard_map/reduce_scatter | solution.py:65
  120.2 0.9 copy-start.2
  120.2 1.1 copy-start.6
  120.2 97.6 %copy-start.1 = (bf16[128,1280]{1,0:T(8,128)(2,1)S(1)}, bf16[128,1280]{1,0:T(8,128)(2,1)}, u32[]{:S(2)}) copy-start(bf16[128,1280]{1,0:T(8,128)(2,1)} %param.21) | copy-start | bytes 983044
  120.2 97.6 %copy-start.9 = (f32[1280]{0:T(1024)S(1)}, f32[1280]{0:T(1024)}, u32[]{:S(2)}) copy-start(f32[1280]{0:T(1024)} %param.28) | copy-start | bytes 15364
  120.2 108.8 %copy-start.14 = (s32[2]{0:T(128)S(1)}, s32[2]{0:T(128)}, u32[]{:S(2)}) copy-start(s32[2]{0:T(128)} %param.29) | copy-start | bytes 28
  120.2 109.1 %copy-start.12 = (s32[2]{0:T(128)S(1)}, s32[2]{0:T(128)}, u32[]{:S(2)}) copy-start(s32[2]{0:T(128)} %param.30) | copy-start | bytes 28
  120.2 177.4 %all-gather.8.cloned.1.call-start = ((), (), s32[]{:S(2)}) async-start(), calls=%async_computation.5 | async-start | bytes 4456448 | tf_op jit(solution)/shard_map/all_gather | solution.py:96
  122.9 262.9 %all-gather.6.cloned.1.call-start = ((), (), s32[]{:S(2)}) async-start(), calls=%async_computation.4 | async-start | bytes 5570560 | tf_op jit(solution)/shard_map/all_gather | solution.py:76
  219.5 83.4 %copy-start.4 = (bf16[128,1280]{1,0:T(8,128)(2,1)}, bf16[128,1280]{1,0:T(8,128)(2,1)S(1)}, u32[]{:S(2)}) copy-start(bf16[128,1280]{1,0:T(8,128)(2,1)S(1)} %minimum_convert_fusion.2) | copy-start | bytes 983044
  219.5 8.7 %collective-permute-start = (bf16[128,1280]{1,0:T(8,128)(2,1)S(1)}, bf16[128,1280]{1,0:T(8,128)(2,1)S(1)}, u32[]{:S(2)}, u32[]{:S(2)}) collective-permute-start(bf16[128,1280]{1,0:T(8,128)(2,1)S(1)} %minimum_convert_fusion.2), channel_id=1, source_target_pairs={{0,16},{16,32},{32,48},{48,64},{64,80},{80,96},{96,112},{112,128},... | collective-permute-start | bytes 983048 | tf_op jit(solution)/shard_map/ppermute | solution.py:11
  228.2 0.7 copy-start.5
  228.9 266.8 %reduce-scatter.5.cloned.1.call-start = ((), (), s32[]{:S(2)}) async-start(), calls=%async_computation.6 | async-start | bytes 4456448 | tf_op jit(solution)/shard_map/reduce_scatter | solution.py:121
  229.0 5.3 collective-permute-start.1
  235.0 150.8 %copy-start.13 = (bf16[1280,128]{1,0:T(8,128)(2,1)S(1)}, bf16[1280,128]{1,0:T(8,128)(2,1)}, u32[]{:S(2)}) copy-start(bf16[1280,128]{1,0:T(8,128)(2,1)} %param.31) | copy-start | bytes 983044
  303.1 86.8 %copy-start.11 = (f32[128]{0:T(128)S(1)}, f32[128]{0:T(128)}, u32[]{:S(2)}) copy-start(f32[128]{0:T(128)} %param.36) | copy-start | bytes 1540
  390.9 4.7 copy-start.15
  402.7 1.0 copy-start.3
  402.7 1.0 copy-start.7
  402.7 1.0 copy-start.8
  402.7 172.8 %copy-start.10 = (f32[16,4]{0,1:T(4,128)S(1)}, f32[16,4]{0,1:T(4,128)}, u32[]{:S(2)}) copy-start(f32[16,4]{0,1:T(4,128)} %param.39) | copy-start | bytes 772
Sparse Core Ops, SparseCore 0:
  14.5 90.0 all-gather.3
  120.4 97.3 reduce-scatter.2
  220.8 76.7 all-gather.7
  299.9 85.8 all-gather.5
  402.9 92.8 reduce-scatter.4
where the time goes:
time: 585 us; the launch traced here: 583 us
  waiting for transfers between devices  434 us (74%)
  blocking collectives  74.7 us (13%)
  matrix products  35.9 us (6%)
  between operations  17.3 us (3%)
  other arithmetic  16.3 us (3%)
    reduce_scatter x1, waiting for transfers between devices, local(): lax.psum_scatter(jnp.dot(hidden_c, w_down, preferred_element_type=jnp.flo...  94.3 us
    reduce_scatter x1, waiting for transfers between devices, local(): lax.psum_scatter(jnp.dot(attended, w_out, preferred_element_type=jnp.floa...  91.1 us
    all_gather x1, waiting for transfers between devices, local(): lax.all_gather(normed_c, 'tp', axis=0, tiled=True)  89.6 us
    all_gather x1, waiting for transfers between devices, local(): piece = lax.all_gather(moved, 'tp', axis=0, tiled=True)  82.6 us
    pmax x1, blocking collectives, local(): cur_text = lax.pmax(cur_text, ('grp', 'tp'))  74.7 us
    all_gather x1, waiting for transfers between devices, local(): lax.all_gather(tnormed_c, 'tp', axis=0, tiled=True)  62.6 us
    ppermute x2, waiting for transfers between devices, passed_along(): lax.ppermute(value, axis, [(i, (i + by) % count) for i in range(count)])  13.6 us
  transfers between devices with their start and end apart: 7, of which 7 were waited for; matrix products, arithmetic and copies ran while one was open for 2% of the time, Pallas kernels for 0%

commit v1 on v0

--- a/solution.py
+++ b/solution.py
@@ -1,21 +1,290 @@
+import functools
+
 import jax
 import jax.numpy as jnp
 from jax import lax
+from jax.experimental import pallas as pl
+from jax.experimental.pallas import tpu as pltpu
 from jax.sharding import PartitionSpec as P
 
+MESH = pl.DeviceIdType.MESH
+BF = jnp.bfloat16
+F32 = jnp.float32
 TILES = 4
+ROWS = 128
+ENC = 1280
+SH = 320
+NSEM = 128
+
+
+class Net:
+    def __init__(self, ssem, rsem):
+        self.ssem, self.rsem, self.used, self.sent = ssem, rsem, 0, []
+        g, t = lax.axis_index("grp"), lax.axis_index("tp")
+        self.g, self.t = g, t
+        self.core, self.x, self.zl = g % 2, (g // 2) % 4, g // 8
+        self.y, self.z = t % 4, t // 4
+
+    def peer(self, axis, d):
+        if axis == "y":
+            return (self.g, self.z * 4 + (self.y + d) % 4)
+        if axis == "z":
+            return (self.g, ((self.z + d) % 4) * 4 + self.y)
+        if axis == "x":
+            return ((self.zl * 4 + (self.x + d) % 4) * 2 + self.core, self.t)
+        if axis == "l":
+            return ((self.g + 8) % 16, self.t)
+        if axis == "c":
+            return (self.g + 1 - 2 * self.core, self.t)
+        return ((self.g + axis) % 16, ((self.z + d) % 4) * 4 + self.y)
+
+    def barrier(self, peers):
+        sem = pltpu.get_barrier_semaphore()
+        for axis, d in peers:
+            pl.semaphore_signal(sem, inc=1, device_id=self.peer(axis, d), device_id_type=MESH)
+        pl.semaphore_wait(sem, len(peers))
+
+    def send(self, src, dst, axis, d):
+        k = self.used
+        self.used += 1
+        copy = pltpu.make_async_remote_copy(
+            src_ref=src,
+            dst_ref=dst,
+            send_sem=self.ssem.at[k],
+            recv_sem=self.rsem.at[k],
+            device_id=self.peer(axis, d),
+            device_id_type=MESH,
+        )
+        copy.start()
+        self.sent.append(copy)
+        return copy
+
+    def finish(self):
+        for copy in self.sent:
+            copy.wait_send()
+
+
+def rows_of(start, size, unit=16):
+    return pl.ds(pl.multiple_of(start, unit), size)
+
+
+def total_max(values):
+    return jnp.max(jnp.max(values, axis=0, keepdims=True), axis=1, keepdims=True)
+
+
+def enc_kernel(
+    image, lng, lnb, bup, bdown, hist, wup, wdown,
+    feat_out, cur_out,
+    WU, WD, BU, NB, HB, HM, PS, RX, RY, CUR, CR, lsem, ssem, rsem,
+):
+    net = Net(ssem, rsem)
+    x, c = net.x, net.core
+    net.barrier(
+        [("y", 1), ("y", 2), ("y", 3), ("z", 1), ("z", 2), ("z", 3), ("x", 1), ("x", 2), ("x", 3)]
+        + [("c", 1), ("l", 1)]
+    )
+    own = [
+        pltpu.make_async_copy(wup, WU.at[pl.ds(0, SH)], lsem.at[0]),
+        pltpu.make_async_copy(wdown, WD.at[pl.ds(0, SH)], lsem.at[1]),
+    ]
+    for copy in own:
+        copy.start()
+
+    def mine(ref):
+        return ref.at[rows_of(x * 80, 80), rows_of(c * 640, 640, 128)]
+
+    def part(ref, slot, at):
+        return ref.at[rows_of(slot * SH + at * 80, 80), rows_of(c * 640, 640, 128)]
+
+    def half(ref, slot):
+        return ref.at[pl.ds(slot * SH, SH), rows_of(c * 640, 640, 128)]
+
+    zu = {3: net.send(mine(wup), part(WU, 3, x), "z", 1), 1: net.send(mine(wup), part(WU, 1, x), "z", 3)}
+    zd = {3: net.send(mine(wdown), part(WD, 3, x), "z", 1), 1: net.send(mine(wdown), part(WD, 1, x), "z", 3)}
+    BU[0] = bup[...]
+    zb = [net.send(bup, BU.at[(4 - d) % 4], "z", d) for d in (1, 2, 3)]
+
+    limits = jnp.max(hist[...], axis=0, keepdims=True)
+    lim = [limits[:, i : i + 1] for i in range(4)]
+
+    image_f = image[...].astype(F32)
+    centred = image_f - jnp.mean(image_f, axis=-1, keepdims=True)
+    spread = jnp.mean(centred * centred, axis=-1, keepdims=True)
+    normed = centred * lax.rsqrt(spread + 1e-05) * lng[...] + lnb[...]
+    cur0 = total_max(jnp.abs(normed))
+    NB[0] = jnp.clip(normed, -lim[0], lim[0]).astype(BF)
+    nb3 = net.send(NB.at[0], NB.at[3], "y", 1)
+    nb1 = net.send(NB.at[0], NB.at[1], "y", 3)
+
+    lo, hi = pl.ds(0, 640), pl.ds(640, 640)
+
+    def spread_x(ref, slot):
+        return (
+            net.send(part(ref, slot, x), part(ref, slot, x), "x", 1),
+            net.send(part(ref, slot, x), part(ref, slot, x), "x", 3),
+        )
+
+    xu, xd = {}, {}
+    zu[3].wait_recv()
+    zu[2] = net.send(part(WU, 3, x), part(WU, 2, x), "z", 1)
+    xu[3] = spread_x(WU, 3)
+    zu[1].wait_recv()
+    xu[1] = spread_x(WU, 1)
+    zd[1].wait_recv()
+    zd[2] = net.send(part(WD, 1, x), part(WD, 2, x), "z", 3)
+    xd[1] = spread_x(WD, 1)
+    zd[3].wait_recv()
+    xd[3] = spread_x(WD, 3)
+
+    nb3.wait_recv()
+    nb2a = net.send(NB.at[3, :, lo], NB.at[2, :, lo], "y", 1)
+    nb1.wait_recv()
+    nb2b = net.send(NB.at[1, :, hi], NB.at[2, :, hi], "y", 3)
+
+    left, right = (x + 3) % 4, (x + 1) % 4
+    xf = {}
+
+    def on_u(slot):
+        xu[slot][0].wait_recv()
+        xf["u", slot] = net.send(part(WU, slot, left), part(WU, slot, left), "x", 1)
+
+    def on_d(slot):
+        xd[slot][1].wait_recv()
+        xf["d", slot] = net.send(part(WD, slot, right), part(WD, slot, right), "x", 3)
+
+    def core_u(slot):
+        xu[slot][1].wait_recv()
+        xf["u", slot].wait_recv()
+        return net.send(half(WU, slot), half(WU, slot), "c", 1)
+
+    def core_d(slot):
+        xd[slot][0].wait_recv()
+        xf["d", slot].wait_recv()
+        return net.send(half(WD, slot), half(WD, slot), "c", 1)
+
+    on_u(3)
+    zu[2].wait_recv()
+    xu[2] = spread_x(WU, 2)
+    on_u(1)
+    on_d(1)
+    zd[2].wait_recv()
+    xd[2] = spread_x(WD, 2)
+    cu1 = core_u(1)
+    on_d(3)
+    on_u(2)
+    cu3 = core_u(3)
+    nb2a.wait_recv()
+    nb2b.wait_recv()
+    own[0].wait()
+    for copy in zb:
+        copy.wait_recv()
+    on_d(2)
+    cu2 = core_u(2)
+    cu1.wait_recv()
+
+    HM[...] = jnp.zeros_like(HM)
+
+    def up(pair):
+        rows = pl.ds(pair * 640, 640)
+        bias = jnp.concatenate([BU[2 * pair][0:1, :SH], BU[2 * pair + 1][0:1, :SH]], axis=1)
+
+        def step(i, carry):
+            pre = lax.dot_general(
+                NB[i], WU[rows, :], (((1,), (1,)), ((), ())), preferred_element_type=F32
+            )
+            pre = pre + bias
+            hidden = 0.5 * pre * (1.0 + lax.erf(pre * (0.5**0.5)))
+            HM[...] = jnp.maximum(HM[...], jnp.max(jnp.abs(hidden), axis=0, keepdims=True))
+            HB[i, :, rows] = jnp.clip(hidden, -lim[1], lim[1]).astype(BF)
+            return carry
+
+        lax.fori_loop(0, 4, step, 0)
+
+    up(0)
+    cu2.wait_recv()
+    cu3.wait_recv()
+    cds = [core_d(1), core_d(3), core_d(2)]
+    up(1)
+    own[1].wait()
+    for copy in cds:
+        copy.wait_recv()
+
+    def down(i):
+        return jnp.dot(HB[i], WD[...], preferred_element_type=F32)
+
+    PS[0] = down(2).astype(BF)
+    rx0 = net.send(PS.at[0, :, lo], RX.at[0], "y", 1)
+    rx1 = net.send(PS.at[0, :, hi], RX.at[1], "y", 3)
+    plus = down(1)
+    PS[1, :, hi] = plus[:, 640:].astype(BF)
+    rx0.wait_recv()
+    PS[1, :, lo] = (plus[:, :640] + RX[0].astype(F32)).astype(BF)
+    ry0 = net.send(PS.at[1], RY.at[0], "y", 1)
+    minus = down(3)
+    PS[2, :, lo] = minus[:, :640].astype(BF)
+    rx1.wait_recv()
+    PS[2, :, hi] = (minus[:, 640:] + RX[1].astype(F32)).astype(BF)
+    ry1 = net.send(PS.at[2], RY.at[1], "y", 3)
+    feature = image[...].astype(F32) + bdown[...] + down(0)
+    ry0.wait_recv()
+    feature = feature + RY[0].astype(F32)
+    ry1.wait_recv()
+    feature = feature + RY[1].astype(F32)
+    cur2 = total_max(jnp.abs(feature))
+    feat_out[...] = jnp.clip(feature, -lim[2], lim[2]).astype(BF)
+
+    cur1 = total_max(HM[...])
+    lane = lax.broadcasted_iota(jnp.int32, (8, 128), 1)
+    cur = jnp.where(lane == 0, cur0, 0.0) + jnp.where(lane == 1, cur1, 0.0)
+    cur = cur + jnp.where(lane == 2, cur2, 0.0)
+    for i, (axis, ds) in enumerate((("c", (1,)), ("y", (1, 2, 3)), ("x", (1, 2, 3)), ("z", (1, 2, 3)), ("l", (1,)))):
+        CUR[i] = cur
+        got = [net.send(CUR.at[i], CR.at[i, j], axis, d) for j, d in enumerate(ds)]
+        for j, copy in enumerate(got):
+            copy.wait_recv()
+            cur = jnp.maximum(cur, CR[i, j])
+    cur_out[...] = cur
+    net.finish()
+
+
+def encoder(image, ln_gain, ln_bias, b_up, b_down, amax_hist, w_up, w_down):
+    vm = pl.BlockSpec(memory_space=pltpu.VMEM)
+    hbm = pl.BlockSpec(memory_space=pl.ANY)
+    bup = jnp.pad(b_up[None, :], ((0, 7), (0, 64)))
+    return pl.pallas_call(
+        enc_kernel,
+        out_shape=(
+            jax.ShapeDtypeStruct((ROWS, ENC), BF),
+            jax.ShapeDtypeStruct((8, 128), F32),
+        ),
+        in_specs=[vm] * 6 + [hbm] * 2,
+        out_specs=(vm, vm),
+        scratch_shapes=[
+            pltpu.VMEM((4 * SH, ENC), BF),
+            pltpu.VMEM((4 * SH, ENC), BF),
+            pltpu.VMEM((4, 8, 384), F32),
+            pltpu.VMEM((4, ROWS, ENC), BF),
+            pltpu.VMEM((4, ROWS, 4 * SH), BF),
+            pltpu.VMEM((1, 640), F32),
+            pltpu.VMEM((3, ROWS, ENC), BF),
+            pltpu.VMEM((2, ROWS, 640), BF),
+            pltpu.VMEM((2, ROWS, ENC), BF),
+            pltpu.VMEM((5, 8, 128), F32),
+            pltpu.VMEM((5, 3, 8, 128), F32),
+            pltpu.SemaphoreType.DMA((4,)),
+            pltpu.SemaphoreType.DMA((NSEM,)),
+            pltpu.SemaphoreType.DMA((NSEM,)),
+        ],
+        compiler_params=pltpu.CompilerParams(
+            collective_id=0, has_side_effects=True, vmem_limit_bytes=56 << 20
+        ),
+        name="encoder",
+    )(image, ln_gain[None, :], ln_bias[None, :], bup, b_down[None, :], amax_hist, w_up.T, w_down)
 
 
 def passed_along(value, axis, by):
     count = lax.axis_size(axis)
     return lax.ppermute(value, axis, [(i, (i + by) % count) for i in range(count)])
-
-
-def layer_norm(values, gain, bias):
-    centre = jnp.mean(values, axis=-1, keepdims=True)
-    centred = values - centre
-    spread = jnp.mean(centred * centred, axis=-1, keepdims=True)
-    return centred * lax.rsqrt(spread + 1e-05) * gain + bias
 
 
 def rms_norm(values, gain, small):
@@ -45,33 +314,7 @@
 ):
     limits = jnp.max(amax_hist, axis=0)
     head_dim = k_gain.shape[0]
-    image_f = image.astype(jnp.float32)
-    normed = layer_norm(image_f, ln_gain, ln_bias)
-    cur_input = jnp.max(jnp.abs(normed))
-    cur_input = lax.pmax(cur_input, ("grp", "tp"))
-    normed_c = jnp.clip(normed, -limits[0], limits[0]).astype(jnp.bfloat16)
-    hidden = jax.nn.gelu(
-        jnp.dot(
-            lax.all_gather(normed_c, "tp", axis=0, tiled=True),
-            w_up,
-            preferred_element_type=jnp.float32,
-        )
-        + b_up,
-        approximate=False,
-    )
-    cur_hidden = jnp.max(jnp.abs(hidden))
-    cur_hidden = lax.pmax(cur_hidden, ("grp", "tp"))
-    hidden_c = jnp.clip(hidden, -limits[1], limits[1]).astype(jnp.bfloat16)
-    summed = lax.psum_scatter(
-        jnp.dot(hidden_c, w_down, preferred_element_type=jnp.float32).astype(jnp.bfloat16),
-        "tp",
-        scatter_dimension=0,
-        tiled=True,
-    ).astype(jnp.float32)
-    feature = image_f + summed + b_down
-    cur_feature = jnp.max(jnp.abs(feature))
-    cur_feature = lax.pmax(cur_feature, ("grp", "tp"))
-    features = jnp.clip(feature, -limits[2], limits[2]).astype(jnp.bfloat16)
+    features, cur = encoder(image, ln_gain, ln_bias, b_up, b_down, amax_hist, w_up, w_down)
     moved, counts = passed_along((features, tile_count), "grp", 1)
     piece = lax.all_gather(moved, "tp", axis=0, tiled=True)
     projected = jnp.concatenate(
@@ -125,32 +368,15 @@
         tiled=True,
     ).astype(jnp.float32)
     mixed = (text_f + jnp.tanh(attn_gate[0]) * total).astype(jnp.bfloat16)
-    current = jnp.stack([cur_input, cur_hidden, cur_feature, cur_text])
+    current = jnp.concatenate([cur[0, :3], cur_text[None]])
     amax_next = jnp.concatenate([current[None, :], amax_hist[:-1]], axis=0)
     return (mixed, features, amax_next)
 
 
 def solution(mesh):
+    rows = P(("grp", "tp"), None)
     in_specs = (
-        P(("grp", "tp"), None),
-        P(("grp", "tp"), None),
-        P(),
-        P(),
-        P(None, "tp"),
-        P("tp"),
-        P("tp", None),
-        P(),
-        P("grp"),
-        P("grp"),
-        P(None, "tp"),
-        P(None, "tp"),
-        P(),
-        P(None, "tp"),
-        P(),
-        P(),
-        P("tp", None),
-        P(),
-        P(),
-    )
-    out_specs = (P(("grp", "tp"), None), P(("grp", "tp"), None), P())
-    return jax.shard_map(local, mesh=mesh, in_specs=in_specs, out_specs=out_specs, check_vma=False)
+        rows, rows, P(), P(), P(None, "tp"), P("tp"), P("tp", None), P(), P("grp"), P("grp"),
+        P(None, "tp"), P(None, "tp"), P(), P(None, "tp"), P(), P(), P("tp", None), P(), P(),
+    )
+    return jax.shard_map(local, mesh=mesh, in_specs=in_specs, out_specs=(rows, rows, P()), check_vma=False)

time: 585 us -> 404 us (0.69)
  waiting for transfers between devices: 434 us -> 175 us
  Pallas kernels: 0 us -> 93.9 us
  matrix products: 35.9 us -> 20.5 us
  local copies, waits for them, and re-layouts: 4.22 us -> 11.7 us
  other arithmetic: 16.3 us -> 9.98 us
    reduce_scatter x1 -> x0, waiting for transfers between devices: 94.3 us -> none  [local(): lax.psum_scatter(jnp.dot(hidden_c, w_down, preferred_element_type=jnp.flo...]
    pallas_call x0 -> x1, Pallas kernels: none -> 93.9 us  [encoder(): pl.pallas_call(enc_kernel, out_shape=(jax.ShapeDtypeStruct((ROWS, ENC), B...]
    all_gather x1 -> x0, waiting for transfers between devices: 89.6 us -> none  [local(): lax.all_gather(normed_c, 'tp', axis=0, tiled=True)]
    all_gather x1, waiting for transfers between devices: 62.6 us -> 0.01 us  [local(): lax.all_gather(tnormed_c, 'tp', axis=0, tiled=True)]
    dot_general x2 -> x0, matrix products: 15.6 us -> none  [the longest x1 10.2 us: local(): jnp.dot(lax.all_gather(normed_c, 'tp', axis=0, tiled=True), w_up, preferr...]
    all_gather x1, waiting for transfers between devices: 82.6 us -> 70.2 us  [local(): piece = lax.all_gather(moved, 'tp', axis=0, tiled=True)]
  transfers between devices with their start and end apart: 7 -> 5, of which waited for: 7 -> 4; matrix products, arithmetic and copies ran while one was open for 2% -> 4% of each run, Pallas kernels for 0% -> 23%
where the time goes in v1:
time: 404 us; the launch traced here: 401 us
  waiting for transfers between devices  175 us (43%)
  Pallas kernels  93.9 us (23%)
  blocking collectives  74.6 us (18%)
  matrix products  20.5 us (5%)
  between operations  15.3 us (4%)
  local copies, waits for them, and re-layouts  11.7 us (3%)
  other arithmetic  9.98 us (2%)
    pallas_call x1, Pallas kernels, encoder(): pl.pallas_call(enc_kernel, out_shape=(jax.ShapeDtypeStruct((ROWS, ENC), B...  93.9 us
    reduce_scatter x1, waiting for transfers between devices, local(): lax.psum_scatter(jnp.dot(attended, w_out, preferred_element_type=jnp.floa...  91.2 us
    pmax x1, blocking collectives, local(): cur_text = lax.pmax(cur_text, ('grp', 'tp'))  74.6 us
    all_gather x1, waiting for transfers between devices, local(): piece = lax.all_gather(moved, 'tp', axis=0, tiled=True)  70.2 us
    ppermute x2, waiting for transfers between devices, passed_along(): lax.ppermute(value, axis, [(i, (i + by) % count) for i in range(count)])  13.3 us
  transfers between devices with their start and end apart: 5, of which 4 were waited for; matrix products, arithmetic and copies ran while one was open for 4% of the time, Pallas kernels for 23%

profile of v1, /device:TPU:40, one launch (start us, length us, event | category | flops | bytes accessed | tf_op | source)
XLA Modules:
  0.0 401.3 jit_solution(2630024651253096349)
XLA Ops:
  7.2 0.0 copy-start
  7.2 0.0 all-gather.5.cloned.1.call-start
  7.2 1.2 fusion.3
  8.4 0.8 reduce_max.18
  9.2 0.6 slice.10
  10.4 2.5 fusion.8
  12.9 0.0 all-gather.5.cloned.1.call-update
  12.9 0.0 all-gather.3.cloned.1.call-start
  13.0 1.4 copy.26.hist
  14.3 0.7 broadcast_in_dim.42
  15.0 1.3 broadcast_in_dim.40.lng
  16.3 1.3 broadcast_in_dim.41.lnb
  17.6 1.3 broadcast_in_dim.43.bdown
  18.9 0.6 pad.4.bup
  19.5 93.9 %encoder.1 = (bf16[128,1280]{1,0:T(8,128)(2,1)}, f32[8,128]{1,0:T(8,128)}) custom-call(bf16[128,1280]{1,0:T(8,128)(2,1)} %image.1, f32[1,1280]{1,0:T(1,128)} %broadcast_in_dim.40.lng, f32[1,1280]{1,0:T(1,128)} %broadcast_in_dim.41.lnb, f32[8,384]{1,0:T(8,128)} %pad.4.bup, f32[1,1280]{1,0:T(1,128)} %broadcast_in_dim.43.bdown, f32[16,4]{1,0:T(8,128)} %copy.26.hist, ...), custom_call_target="tpu_custom_call" | custom-call | tf_op jit(solution)/shard_map/encoder/pallas_call | solution.py:254
  113.4 0.1 collective-permute-start
  113.5 8.8 %collective-permute-done = bf16[128,1280]{1,0:T(8,128)(2,1)S(1)} collective-permute-done((bf16[128,1280]{1,0:T(8,128)(2,1)}, bf16[128,1280]{1,0:T(8,128)(2,1)S(1)}, u32[]{:S(2)}, u32[]{:S(2)}) %collective-permute-start) | collective-permute-done | bytes 327712 | tf_op jit(solution)/shard_map/ppermute | solution.py:287
  122.3 0.0 copy-start.3
  122.3 0.7 copy-done.3
  123.0 0.0 all-gather.3.cloned.1.call-update
  123.1 0.0 reduce-scatter.2.cloned.1.call-start
  123.1 0.3 collective-permute-start.1
  123.4 0.7 compare_select_fusion
  124.1 4.5 %collective-permute-done.1 = s32[2]{0:T(128)S(1)} collective-permute-done((s32[2]{0:T(128)}, s32[2]{0:T(128)S(1)}, u32[]{:S(2)}, u32[]{:S(2)}) %collective-permute-start.1) | collective-permute-done | bytes 40 | tf_op jit(solution)/shard_map/ppermute | solution.py:287
  128.6 0.6 gather_fusion
  129.2 0.7 select_multiply_fusion
  129.9 0.1 compare_convert_fusion
  130.0 0.0 all-gather.5.cloned.1.call-done
  130.0 5.5 %bitcast_reduce_fusion.1 = (f32[256,2]{0,1:T(2,128)S(1)}, f32[256,256]{0,1:T(8,128)S(1)}) fusion(bf16[256,8192]{1,0:T(8,128)(2,1)} %all-gather.5.cloned.1.call-done, bf16[8192,256]{1,0:T(8,128)(2,1)} %param.34), kind=kOutput, calls=%fused_computation.31 | convolution fusion | flops 1073872384 | bytes 8652800 | tf_op jit(solution)/shard_map/dot_general | solution.py:338
  135.4 0.0 copy-start.6
  135.5 0.1 reshape.90
  135.6 0.1 copy.27
  135.8 0.0 copy-start.7
  135.8 70.2 %all-gather.3.cloned.1.call-done = bf16[2048,1280]{1,0:T(8,128)(2,1)} async-done(((bf16[128,1280]{1,0:T(8,128)(2,1)}), bf16[2048,1280]{1,0:T(8,128)(2,1)}) %all-gather.3.cloned.1.call-update) | async-done | bytes 5242896 | tf_op jit(solution)/shard_map/all_gather | solution.py:319
  206.0 0.0 copy-done
  206.0 4.1 %multiply_reduce_fusion = (f32[2048]{0:T(1024)S(1)}, f32[2048,128]{1,0:T(8,128)S(1)}) fusion(bf16[2048,1280]{1,0:T(8,128)(2,1)} %all-gather.3.cloned.1.call-done, bf16[1280,128]{1,0:T(8,128)(2,1)S(1)} %copy-done), kind=kOutput, calls=%fused_computation.12 | convolution fusion | flops 671610880 | bytes 6627328 | tf_op jit(solution)/shard_map/dot_general | solution.py:322
  210.1 0.0 copy-done.6
  210.1 0.3 multiply_convert_fusion
  210.5 0.6 gather_fusion.2
  211.1 0.0 copy-done.7
  211.1 0.0 copy-start.8
  211.1 4.0 %convolution_convert_fusion.1 = bf16[2048,128]{1,0:T(8,128)(2,1)S(1)} fusion(bf16[2048,1280]{1,0:T(8,128)(2,1)} %all-gather.3.cloned.1.call-done, bf16[1280,128]{1,0:T(8,128)(2,1)S(1)} %copy-done.7), kind=kOutput, calls=%fused_computation.4 | convolution fusion | flops 671350784 | bytes 6094848 | tf_op jit(solution)/shard_map/dot_general | solution.py:323
  215.2 0.6 gather_fusion.1
  215.8 0.0 copy-done.8
  215.8 0.7 bitcast_reduce_fusion
  216.5 0.8 fusion.1
  217.3 0.1 copy.30
  217.5 5.4 %convolution_convert_fusion = bf16[256,8192]{1,0:T(8,128)(2,1)} fusion(bf16[256,8192]{1,0:T(8,128)(2,1)} %param.37, bf16[32,8,2,128]{3,2,1,0:T(2,128)(2,1)S(1)} %bitcast.51), kind=kOutput, calls=%fused_computation.3 | convolution fusion | flops 1075838976 | bytes 8519680 | tf_op jit(solution)/shard_map/dot_general | solution.py:365
  222.9 0.0 copy-start.4
  222.9 0.0 copy-start.5
  222.9 0.0 copy-start.2
  222.9 0.0 reduce-scatter.2.cloned.1.call-update
  223.6 0.7 slice_bitcast_fusion
  224.3 91.2 %reduce-scatter.2.cloned.1.call-done = bf16[16,8192]{1,0:T(8,128)(2,1)} async-done(((bf16[256,8192]{1,0:T(8,128)(2,1)}), bf16[16,8192]{1,0:T(8,128)(2,1)}) %reduce-scatter.2.cloned.1.call-update) | async-done | bytes 262160 | tf_op jit(solution)/shard_map/reduce_scatter | solution.py:364
  315.6 0.0 copy-done.1
  315.6 0.0 copy-done.4
  315.6 2.4 fusion.9
  318.0 74.6 %pmax.7 = f32[1]{0:T(128)} all-reduce(f32[1]{0:T(128)} %bitcast.13), channel_id=1, replica_groups=mesh['grp'=16,'tp'=16] {'grp','tp'}, use_global_device_ids=true, to_apply=%region_7.9 | all-reduce | flops 1 | bytes 8 | tf_op jit(solution)/shard_map/pmax | solution.py:336
  392.5 0.7 maximum_bitcast_fusion
  393.3 0.1 copy.31
  393.4 0.0 copy-done.5
  393.4 0.7 pad_maximum_fusion
  394.0 0.0 copy-done.2
  394.0 0.7 copy.44
  (5 shorter events, 0.0 us)
Async XLA Ops:
  7.2 198.8 %copy-start = (bf16[1280,128]{1,0:T(8,128)(2,1)S(1)}, bf16[1280,128]{1,0:T(8,128)(2,1)}, u32[]{:S(2)}) copy-start(bf16[1280,128]{1,0:T(8,128)(2,1)} %param.31) | copy-start | bytes 983044
  7.2 122.8 %all-gather.5.cloned.1.call-start = ((), (), s32[]{:S(2)}) async-start(), calls=%async_computation.2 | async-start | bytes 4456448 | tf_op jit(solution)/shard_map/all_gather | solution.py:339
  12.9 193.1 %all-gather.3.cloned.1.call-start = ((), (), s32[]{:S(2)}) async-start(), calls=%async_computation.1 | async-start | bytes 5570560 | tf_op jit(solution)/shard_map/all_gather | solution.py:319
  113.4 8.9 %collective-permute-start = (bf16[128,1280]{1,0:T(8,128)(2,1)}, bf16[128,1280]{1,0:T(8,128)(2,1)S(1)}, u32[]{:S(2)}, u32[]{:S(2)}) collective-permute-start(bf16[128,1280]{1,0:T(8,128)(2,1)} %get-tuple-element.22), channel_id=1, source_target_pairs={{0,16},{16,32},{32,48},{48,64},{64,80},{80,96},{96,112},{112,128},... | collective-permute-start | bytes 983048 | tf_op jit(solution)/shard_map/ppermute | solution.py:287
  122.3 0.7 copy-start.3
  123.1 192.5 %reduce-scatter.2.cloned.1.call-start = ((), (), s32[]{:S(2)}) async-start(), calls=%async_computation.3 | async-start | bytes 4456448 | tf_op jit(solution)/shard_map/reduce_scatter | solution.py:364
  123.1 5.5 %collective-permute-start.1 = (s32[2]{0:T(128)}, s32[2]{0:T(128)S(1)}, u32[]{:S(2)}, u32[]{:S(2)}) collective-permute-start(s32[2]{0:T(128)} %param.29), channel_id=1, source_target_pairs={{0,16},{16,32},{32,48},{48,64},{64,80},{80,96},{96,112},{112,128},... | collective-permute-start | bytes 32 | tf_op jit(solution)/shard_map/ppermute | solution.py:287
  135.4 74.7 %copy-start.6 = (f32[128]{0:T(128)S(1)}, f32[128]{0:T(128)}, u32[]{:S(2)}) copy-start(f32[128]{0:T(128)} %param.36) | copy-start | bytes 1540
  135.8 75.4 %copy-start.7 = (bf16[1280,128]{1,0:T(8,128)(2,1)S(1)}, bf16[1280,128]{1,0:T(8,128)(2,1)}, u32[]{:S(2)}) copy-start(bf16[1280,128]{1,0:T(8,128)(2,1)} %param.32) | copy-start | bytes 983044
  211.1 4.7 %copy-start.8 = (f32[128]{0:T(128)S(1)}, f32[128]{0:T(128)}, u32[]{:S(2)}) copy-start(f32[128]{0:T(128)} %param.35) | copy-start | bytes 1540
  222.9 92.7 %copy-start.1 = (bf16[16,8192]{1,0:T(8,128)(2,1)S(1)}, bf16[16,8192]{1,0:T(8,128)(2,1)}, u32[]{:S(2)}) copy-start(bf16[16,8192]{1,0:T(8,128)(2,1)} %param.22) | copy-start | bytes 786436
  222.9 92.7 %copy-start.4 = (f32[8192]{0:T(1024)S(1)}, f32[8192]{0:T(1024)}, u32[]{:S(2)}) copy-start(f32[8192]{0:T(1024)} %param.33) | copy-start | bytes 98308
  222.9 170.5 %copy-start.5 = (f32[16,4]{0,1:T(4,128)S(1)}, f32[16,4]{0,1:T(4,128)}, u32[]{:S(2)}) copy-start(f32[16,4]{0,1:T(4,128)} %param.39) | copy-start | bytes 772
  222.9 171.1 %copy-start.2 = (bf16[128,1280]{1,0:T(8,128)(2,1)S(1)}, bf16[128,1280]{1,0:T(8,128)(2,1)}, u32[]{:S(2)}) copy-start(bf16[128,1280]{1,0:T(8,128)(2,1)} %get-tuple-element.22) | copy-start | bytes 983044
Sparse Core Ops, SparseCore 0:
  13.1 87.5 all-gather.4
  123.2 82.7 all-gather.2
  223.0 92.4 reduce-scatter.1

commit v2 on v1

v2 whole, which is shorter than its diff:
```python
import functools

import jax
import jax.numpy as jnp
from jax import lax
from jax.experimental import pallas as pl
from jax.experimental.pallas import tpu as pltpu
from jax.sharding import PartitionSpec as P

MESH = pl.DeviceIdType.MESH
BF = jnp.bfloat16
F32 = jnp.float32
D = 8192
ROWS = 128
ENC = 1280
SH = 320
NSEM = 176


class Net:
    def __init__(self, ssem, rsem):
        self.ssem, self.rsem, self.used, self.sent = ssem, rsem, 0, []
        g, t = lax.axis_index("grp"), lax.axis_index("tp")
        self.g, self.t = g, t
        self.core, self.x, self.zl = g % 2, (g // 2) % 4, g // 8
        self.y, self.z = t % 4, t // 4

    def peer(self, axis, d):
        if axis == "y":
            return (self.g, self.z * 4 + (self.y + d) % 4)
        if axis == "z":
            return (self.g, ((self.z + d) % 4) * 4 + self.y)
        if axis == "x":
            return ((self.zl * 4 + (self.x + d) % 4) * 2 + self.core, self.t)
        if axis == "l":
            return ((self.g + 8) % 16, self.t)
        if axis == "c":
            return (self.g + 1 - 2 * self.core, self.t)
        return ((self.g + axis) % 16, ((self.z + d) % 4) * 4 + self.y)

    def barrier(self, peers):
        sem = pltpu.get_barrier_semaphore()
        for axis, d in peers:
            pl.semaphore_signal(sem, inc=1, device_id=self.peer(axis, d), device_id_type=MESH)
        pl.semaphore_wait(sem, len(peers))

    def send(self, src, dst, axis, d):
        k = self.used
        self.used += 1
        copy = pltpu.make_async_remote_copy(
            src_ref=src,
            dst_ref=dst,
            send_sem=self.ssem.at[k],
            recv_sem=self.rsem.at[k],
            device_id=self.peer(axis, d),
            device_id_type=MESH,
        )
        copy.start()
        self.sent.append(copy)
        return copy

    def finish(self):
        for copy in self.sent:
            copy.wait_send()


def rows_of(start, size, unit=16):
    return pl.ds(pl.multiple_of(start, unit), size)


def total_max(values):
    return jnp.max(jnp.max(values, axis=0, keepdims=True), axis=1, keepdims=True)


def kernel(
    image, text, lng, lnb, bup, bdown, tiles, assign, ing, qg, kg, gate, hist,
    wup, wdown, wkey, wvalue, wquery, wout,
    mixed_out, feat_out, amax_out,
    WU, WD, WK, WV, WO, WQ, BU, NB, HB, HM, PF, PS, RX, RY, CUR, CR,
    T, QA, QO, QB, AS, FB, KB, VB, MK, AS2, AN, AD, AT, ADT, DN, G, OF, OS, OX, OY, FS, MX,
    lsem, ssem, rsem,
):
    net = Net(ssem, rsem)
    x, y, z, c = net.x, net.y, net.z, net.core
    net.barrier(
        [("y", 1), ("y", 2), ("y", 3), ("z", 1), ("z", 2), ("z", 3), ("x", 1), ("x", 2), ("x", 3)]
        + [("c", 1), ("l", 1)]
        + [(by, d) for by in (1, -1) for d in range(4)]
    )

    def up_part(ref, slot, at):
        return ref.at[rows_of(slot * SH + at * 80, 80), rows_of(c * 640, 640, 128)]

    def up_half(ref, slot):
        return ref.at[pl.ds(slot * SH, SH), rows_of(c * 640, 640, 128)]

    def kv_part(ref, slot, at):
        return ref.at[rows_of(c * 640 + at * 160, 160), pl.ds(slot * 128, 128)]

    def kv_half(ref, slot):
        return ref.at[rows_of(c * 640, 640), pl.ds(slot * 128, 128)]

    def wo_part(slot, at):
        return WO.at[rows_of(slot * 256 + at * 64, 64), rows_of(c * 1024, 1024, 128)]

    def wo_half(slot):
        return WO.at[pl.ds(slot * 256, 256), rows_of(c * 1024, 1024, 128)]

    left, right = (x + 3) % 4, (x + 1) % 4

    class Gather:
        def __init__(self, ref, source, part, half, forward):
            self.ref, self.part, self.half, self.forward = ref, part, half, forward
            self.zs, self.xs, self.fs, self.cs = {}, {}, {}, {}
            self.zs[3] = net.send(source, part(ref, 3, x), "z", 1)
            self.zs[1] = net.send(source, part(ref, 1, x), "z", 3)

        def z_got(self, slot):
            self.zs[slot].wait_recv()
            if slot == (3 if self.forward > 0 else 1):
                d = 1 if self.forward > 0 else 3
                self.zs[2] = net.send(self.part(self.ref, slot, x), self.part(self.ref, 2, x), "z", d)
            mine = self.part(self.ref, slot, x)
            self.xs[slot] = [net.send(mine, mine, "x", d) for d in (1, 3)]

        def x_got(self, slot):
            if self.forward > 0:
                self.xs[slot][0].wait_recv()
                other = self.part(self.ref, slot, left)
                self.fs[slot] = net.send(other, other, "x", 1)
            else:
                self.xs[slot][1].wait_recv()
                other = self.part(self.ref, slot, right)
                self.fs[slot] = net.send(other, other, "x", 3)

        def swap(self, slot):
            self.xs[slot][1 if self.forward > 0 else 0].wait_recv()
            self.fs[slot].wait_recv()
            mine = self.half(self.ref, slot)
            self.cs[slot] = net.send(mine, mine, "c", 1)

        def ready(self, *slots):
            for slot in slots:
                self.cs[slot].wait_recv()

    own = [
        pltpu.make_async_copy(wup, WU.at[pl.ds(0, SH)], lsem.at[0]),
        pltpu.make_async_copy(wdown, WD.at[pl.ds(0, SH)], lsem.at[1]),
        pltpu.make_async_copy(wkey, WK.at[:, pl.ds(0, 128)], lsem.at[2]),
        pltpu.make_async_copy(wvalue, WV.at[:, pl.ds(0, 128)], lsem.at[3]),
        pltpu.make_async_copy(
            wout.at[:, rows_of(z * 2048, 2048, 128)], WO.at[pl.ds(0, 256)], lsem.at[4]
        ),
        pltpu.make_async_copy(wquery, WQ, lsem.at[5]),
    ]
    for copy in own:
        copy.start()

    mine = (rows_of(x * 80, 80), rows_of(c * 640, 640, 128))
    gu = Gather(WU, wup.at[mine], up_part, up_half, 1)
    gd = Gather(WD, wdown.at[mine], up_part, up_half, -1)
    BU[0, 0:1, pl.ds(0, SH)] = bup[...].reshape(1, SH)
    zb = [net.send(BU.at[0], BU.at[(4 - d) % 4], "z", d) for d in (1, 2, 3)]

    limits = jnp.max(hist[...], axis=0, keepdims=True)
    lim = [limits[:, i : i + 1] for i in range(4)]

    image_f = image[...].astype(F32)
    centred = image_f - jnp.mean(image_f, axis=-1, keepdims=True)
    spread = jnp.mean(centred * centred, axis=-1, keepdims=True)
    normed = centred * lax.rsqrt(spread + 1e-05) * lng[...].reshape(1, ENC) + lnb[...].reshape(1, ENC)
    cur0 = total_max(jnp.abs(normed))
    NB[0] = jnp.clip(normed, -lim[0], lim[0]).astype(BF)
    nb3 = net.send(NB.at[0], NB.at[3], "y", 1)
    nb1 = net.send(NB.at[0], NB.at[1], "y", 3)

    text_f = text[...].astype(F32)
    tnormed = text_f * lax.rsqrt(jnp.mean(text_f * text_f, axis=-1, keepdims=True) + 1e-05)
    tnormed = tnormed * ing[...].reshape(1, D)
    cur3 = total_max(jnp.abs(tnormed))
    tlo, thi = pl.ds(0, D // 2), pl.ds(D // 2, D // 2)

    def tb(ry, zi):
        return rows_of(ry * 64 + zi * 16, 16)

    T[tb(0, z), :] = jnp.clip(tnormed, -lim[3], lim[3]).astype(BF)

    lane = lax.broadcasted_iota(jnp.int32, (8, 128), 1)
    AS[...] = jnp.where(lane == 0, assign[0], assign[1])
    sent_assign = net.send(AS, AS2, -1, 0)

    gu.z_got(3)
    gu.z_got(1)
    gd.z_got(1)
    gd.z_got(3)

    zl, zr = (z + 3) % 4, (z + 1) % 4
    tz3 = net.send(T.at[tb(0, z)], T.at[tb(0, z)], "z", 1)
    tz1 = net.send(T.at[tb(0, z)], T.at[tb(0, z)], "z", 3)

    lo, hi = pl.ds(0, 640), pl.ds(640, 640)
    nb3.wait_recv()
    nb2a = net.send(NB.at[3, :, lo], NB.at[2, :, lo], "y", 1)
    nb1.wait_recv()
    nb2b = net.send(NB.at[1, :, hi], NB.at[2, :, hi], "y", 3)

    class TextRing:
        def __init__(self, zi):
            self.zi = zi
            own_block = T.at[tb(0, zi)]
            self.a3 = net.send(own_block, T.at[tb(3, zi)], "y", 1)
            self.a1 = net.send(own_block, T.at[tb(1, zi)], "y", 3)

        def relay(self):
            self.a3.wait_recv()
            self.f = [net.send(T.at[tb(3, self.zi), tlo], T.at[tb(2, self.zi), tlo], "y", 1)]
            self.a1.wait_recv()
            self.f.append(net.send(T.at[tb(1, self.zi), thi], T.at[tb(2, self.zi), thi], "y", 3))

        def done(self):
            for copy in self.f:
                copy.wait_recv()

    rings = [TextRing(z)]

    gu.x_got(3)
    gu.z_got(2)
    gu.x_got(1)
    gd.x_got(1)
    gd.z_got(2)
    gu.swap(1)
    gd.x_got(3)
    gu.x_got(2)
    gu.swap(3)
    gk = Gather(WK, wkey.at[rows_of(c * 640 + x * 160, 160), :], kv_part, kv_half, 1)
    gv = Gather(WV, wvalue.at[rows_of(c * 640 + x * 160, 160), :], kv_part, kv_half, -1)
    rings[0].relay()
    nb2a.wait_recv()
    nb2b.wait_recv()
    own[0].wait()
    for copy in zb:
        copy.wait_recv()
    gd.x_got(2)
    gu.swap(2)
    gu.ready(1)
    gd.swap(1)
    gd.swap(3)

    HM[...] = jnp.zeros_like(HM)

    def up(pair):
        units = pl.ds(pair * 640, 640)
        bias = jnp.concatenate([BU[2 * pair][0:1, :SH], BU[2 * pair + 1][0:1, :SH]], axis=1)

        def step(i, carry):
            rows = rows_of(i * 256, 256)
            pre = lax.dot_general(
                NB[pl.ds(i * 2, 2)].reshape(256, ENC), WU[units, :], (((1,), (1,)), ((), ())),
                preferred_element_type=F32,
            )
            pre = pre + bias
            hidden = 0.5 * pre * (1.0 + lax.erf(pre * (0.5**0.5)))
            HM[...] = jnp.maximum(HM[...], jnp.max(jnp.abs(hidden), axis=0, keepdims=True))
            HB[rows, units] = jnp.clip(hidden, -lim[1], lim[1]).astype(BF)
            return carry

        lax.fori_loop(0, 2, step, 0)

    up(0)
    tz3.wait_recv()
    tz2a = net.send(T.at[tb(0, zl), tlo], T.at[tb(0, zl), tlo], "z", 1)
    rings.append(TextRing(zl))
    tz1.wait_recv()
    tz2b = net.send(T.at[tb(0, zr), thi], T.at[tb(0, zr), thi], "z", 3)
    rings.append(TextRing(zr))
    gd.swap(2)
    gu.ready(2, 3)
    up(1)
    own[1].wait()
    gd.ready(1, 2, 3)

    def down(cols):
        PF[...] = jnp.dot(HB[...], WD[:, cols], preferred_element_type=F32)

    down(lo)
    PS[0, :, lo] = PF[pl.ds(256, 128), :].astype(BF)
    rx0 = net.send(PS.at[0, :, lo], RX.at[0], "y", 1)
    PS[2, :, lo] = PF[pl.ds(384, 128), :].astype(BF)
    OWN0 = image[:, lo].astype(F32) + bdown[lo].reshape(1, 640) + PF[pl.ds(0, 128), :]
    plus_lo = PF[pl.ds(128, 128), :]
    down(hi)
    PS[0, :, hi] = PF[pl.ds(256, 128), :].astype(BF)
    rx1 = net.send(PS.at[0, :, hi], RX.at[1], "y", 3)
    PS[1, :, hi] = PF[pl.ds(128, 128), :].astype(BF)
    rx0.wait_recv()
    PS[1, :, lo] = (plus_lo + RX[0].astype(F32)).astype(BF)
    ry0 = net.send(PS.at[1], RY.at[0], "y", 1)
    rx1.wait_recv()
    PS[2, :, hi] = (PF[pl.ds(384, 128), :] + RX[1].astype(F32)).astype(BF)
    ry1 = net.send(PS.at[2], RY.at[1], "y", 3)

    rings[1].relay()
    rings[2].relay()
    tz2a.wait_recv()
    tz2b.wait_recv()
    zo = (z + 2) % 4
    rings.append(TextRing(zo))
    for part in (gk, gv):
        part.z_got(3)
        part.z_got(1)
    wo_zs = {}
    for d in (1, 3, 2):
        cut = rows_of(((z + d) % 4) * 2048 + c * 1024, 1024, 128)
        wo_zs[4 - d] = net.send(wout.at[rows_of(x * 64, 64), cut], wo_part(4 - d, x), "z", d)

    ry0.wait_recv()
    ry1.wait_recv()
    feat_lo = OWN0 + RY[0, :, lo].astype(F32) + RY[1, :, lo].astype(F32)
    feat_hi = image[:, hi].astype(F32) + bdown[hi].reshape(1, 640) + PF[pl.ds(0, 128), :]
    feat_hi = feat_hi + RY[0, :, hi].astype(F32) + RY[1, :, hi].astype(F32)
    cur2 = jnp.maximum(total_max(jnp.abs(feat_lo)), total_max(jnp.abs(feat_hi)))
    FB[0, :, lo] = jnp.clip(feat_lo, -lim[2], lim[2]).astype(BF)
    FB[0, :, hi] = jnp.clip(feat_hi, -lim[2], lim[2]).astype(BF)
    fb3 = net.send(FB.at[0], FB.at[3], "y", 1)
    fb1 = net.send(FB.at[0], FB.at[1], "y", 3)
    feat_out[...] = FB[0]

    cur1 = total_max(HM[...])
    cur = jnp.where(lane == 0, cur0, 0.0) + jnp.where(lane == 1, cur1, 0.0)
    cur = cur + jnp.where(lane == 2, cur2, 0.0) + jnp.where(lane == 3, cur3, 0.0)
    CUR[0] = cur
    stages = (("c", (1,)), ("y", (1, 2, 3)), ("x", (1, 2, 3)), ("z", (1, 2, 3)), ("l", (1,)))

    def max_send(i):
        axis, ds = stages[i]
        return [net.send(CUR.at[i], CR.at[i, j], axis, d) for j, d in enumerate(ds)]

    def max_take(i, copies):
        value = CUR[i]
        for j, copy in enumerate(copies):
            copy.wait_recv()
            value = jnp.maximum(value, CR[i, j])
        CUR[i + 1] = value

    going = max_send(0)

    for part in (gk, gv):
        part.z_got(2)
        part.x_got(3)
        part.x_got(1)

    fb3.wait_recv()
    fb2a = net.send(FB.at[3, :, lo], FB.at[2, :, lo], "y", 1)
    fb1.wait_recv()
    fb2b = net.send(FB.at[1, :, hi], FB.at[2, :, hi], "y", 3)
    max_take(0, going)
    going = max_send(1)

    for part in (gk, gv):
        part.x_got(2)
        part.swap(1)
        part.swap(3)

    rings[3].relay()
    for ring in rings:
        ring.done()
    own[5].wait()
    QA[...] = jnp.zeros_like(QA)

    def query_step(i, carry):
        span = rows_of(i * 1024, 1024, 128)
        QA[...] += jnp.dot(T[:, span], WQ[span, :], preferred_element_type=F32)
        return carry

    lax.fori_loop(0, D // 1024, query_step, 0)
    for h in range(2):
        cols = pl.ds(h * 128, 128)
        q = QA[:, cols]
        q = q * lax.rsqrt(jnp.mean(q * q, axis=-1, keepdims=True) + 1e-06) * qg[...].reshape(1, 128)
        QO[:, cols] = q.astype(BF)
    qs = [net.send(QO, QB.at[(4 - d) % 4], -1, d) for d in range(4)]

    wo_xs, wo_fs, wo_cs = {}, {}, {}
    for slot in (3, 1, 2):
        wo_zs[slot].wait_recv()
        wo_xs[slot] = [net.send(wo_part(slot, x), wo_part(slot, x), "x", d) for d in (1, 3)]

    for part in (gk, gv):
        part.swap(2)
    own[2].wait()
    own[3].wait()
    for part in (gk, gv):
        part.ready(1, 2, 3)
    fb2a.wait_recv()
    fb2b.wait_recv()

    rows_f = FB[...].reshape(512, ENC)
    keys = jnp.dot(rows_f, WK[...], preferred_element_type=F32)
    for r in range(4):
        k = keys[:, r * 128 : (r + 1) * 128]
        k = k * lax.rsqrt(jnp.mean(k * k, axis=-1, keepdims=True) + 1e-06) * kg[...].reshape(1, 128)
        KB[r] = k.astype(BF)
    values = jnp.dot(rows_f, WV[...], preferred_element_type=F32)
    for r in range(4):
        VB[r, :, pl.ds(0, 128)] = values[:, r * 128 : (r + 1) * 128].astype(BF)
        VB[r, :, pl.ds(128, 128)] = jnp.ones((512, 128), BF)

    max_take(1, going)
    going = max_send(2)

    sent_assign.wait_recv()
    count = jnp.where(z < 2, tiles[0], tiles[1]) * 256
    col = lax.broadcasted_iota(jnp.int32, (256, 512), 1)
    row = lax.broadcasted_iota(jnp.int32, (256, 512), 0)
    at = ((z % 2) * 4 + ((y + (col >> 7)) & 3)) * 128 + (col & 127)
    chosen = jnp.where((row & 63) < 32, AS2[0:1, 0:1], AS2[0:1, 1:2])
    MK[...] = jnp.where((at < count) & (chosen == z // 2), 1.0, 0.0)

    for copy in qs:
        copy.wait_recv()
    ats = []
    lane_w = lax.broadcasted_iota(jnp.int32, (256, 128), 1)
    for r in (2, 1, 3, 0):
        dens = []
        for h in range(2):
            cols = pl.ds(h * 128, 128)
            scores = lax.dot_general(
                QB[r, :, cols], KB[r], (((1,), (1,)), ((), ())), preferred_element_type=F32
            )
            weights = (jnp.exp(scores * (128**-0.5)) * MK[...]).astype(BF)
            both = jnp.dot(weights, VB[r], preferred_element_type=F32)
            AN[r, :, cols] = both[:, :128].astype(BF)
            dens.append(both[:, 128:])
        packed = jnp.where(lane_w == 0, dens[0], jnp.where(lane_w == 1, dens[1], 0.0))
        AD[r] = packed.T[0:8, :]
        ats.append(net.send(AN.at[r], AT.at[(4 - r) % 4], 1, r))
        ats.append(net.send(AD.at[r], ADT.at[(4 - r) % 4], 1, r))

    for slot in (3, 1, 2):
        if slot == 1:
            wo_xs[slot][1].wait_recv()
            wo_fs[slot] = net.send(wo_part(slot, right), wo_part(slot, right), "x", 3)
        else:
            wo_xs[slot][0].wait_recv()
            wo_fs[slot] = net.send(wo_part(slot, left), wo_part(slot, left), "x", 1)
    for slot in (3, 1, 2):
        wo_xs[slot][0 if slot == 1 else 1].wait_recv()
        wo_fs[slot].wait_recv()
        wo_cs[slot] = net.send(wo_half(slot), wo_half(slot), "c", 1)

    max_take(2, going)
    going = max_send(3)

    for copy in ats:
        copy.wait_recv()
    DN[...] = jnp.ones_like(DN)
    DN[pl.ds(0, 8), :] = ADT[0] + ADT[1] + ADT[2] + ADT[3]
    den = DN[...].T
    for h in range(2):
        cols = pl.ds(h * 128, 128)
        num = AT[0, :, cols].astype(F32) + AT[1, :, cols].astype(F32)
        num = num + AT[2, :, cols].astype(F32) + AT[3, :, cols].astype(F32)
        G[:, cols] = (num / den[:, h : h + 1]).astype(BF)
    gs = [net.send(G.at[:, pl.ds(0, 256)], G.at[:, pl.ds((4 - d) * 256, 256)], "z", d) for d in (1, 3, 2)]

    own[4].wait()
    for slot in (1, 2, 3):
        wo_cs[slot].wait_recv()
    for copy in gs:
        copy.wait_recv()

    olo, ohi = pl.ds(0, 1024), pl.ds(1024, 1024)
    OF[...] = jnp.dot(G[...], WO[:, olo], preferred_element_type=F32)
    OS[0, :, olo] = OF[pl.ds(128, 64), :].astype(BF)
    ox0 = net.send(OS.at[0, :, olo], OX.at[0], "y", 1)
    OS[2, :, olo] = OF[pl.ds(192, 64), :].astype(BF)
    out_lo = OF[pl.ds(0, 64), :]
    oplus = OF[pl.ds(64, 64), :]
    OF[...] = jnp.dot(G[...], WO[:, ohi], preferred_element_type=F32)
    OS[0, :, ohi] = OF[pl.ds(128, 64), :].astype(BF)
    ox1 = net.send(OS.at[0, :, ohi], OX.at[1], "y", 3)
    OS[1, :, ohi] = OF[pl.ds(64, 64), :].astype(BF)
    ox0.wait_recv()
    OS[1, :, olo] = (oplus + OX[0].astype(F32)).astype(BF)
    oy0 = net.send(OS.at[1], OY.at[0], "y", 1)
    ox1.wait_recv()
    OS[2, :, ohi] = (OF[pl.ds(192, 64), :] + OX[1].astype(F32)).astype(BF)
    oy1 = net.send(OS.at[2], OY.at[1], "y", 3)
    max_take(3, going)
    going = max_send(4)
    oy0.wait_recv()
    oy1.wait_recv()
    FS[:, olo] = (out_lo + OY[0, :, olo].astype(F32) + OY[1, :, olo].astype(F32)).astype(BF)
    FS[:, ohi] = (OF[pl.ds(0, 64), :] + OY[0, :, ohi].astype(F32) + OY[1, :, ohi].astype(F32)).astype(BF)
    fs = {}
    for d in (2, 1, 3):
        fs[4 - d] = net.send(FS.at[rows_of(((z + d) % 4) * 16, 16)], MX.at[4 - d], "z", d)
    max_take(4, going)
    amax_out[0:1, :] = CUR[5][0:1, 0:4]
    amax_out[pl.ds(1, 15), :] = hist[pl.ds(0, 15), :]
    strength = jnp.tanh(jnp.full((1, 128), gate[0], F32))[:, 0:1]
    for r in (0, 1, 3, 2):
        cols = rows_of(((z + r) % 4) * 2048, 2048, 128)
        if r:
            fs[r].wait_recv()
            total = MX[r].astype(F32)
        else:
            total = FS[rows_of(z * 16, 16), :].astype(F32)
        mixed_out[:, cols] = (text[:, cols].astype(F32) + strength * total).astype(BF)
    net.finish()


def local(
    image, text, ln_gain, ln_bias, w_up, b_up, w_down, b_down, tile_count, assign,
    w_key, w_value, in_gain, w_query, q_gain, k_gain, w_out, attn_gate, amax_hist,
):
    vm = pl.BlockSpec(memory_space=pltpu.VMEM)
    sm = pl.BlockSpec(memory_space=pltpu.SMEM)
    hbm = pl.BlockSpec(memory_space=pl.ANY)
    return pl.pallas_call(
        kernel,
        out_shape=(
            jax.ShapeDtypeStruct((16, D), BF),
            jax.ShapeDtypeStruct((ROWS, ENC), BF),
            jax.ShapeDtypeStruct((16, 4), F32),
        ),
        in_specs=[vm] * 6 + [sm] * 2 + [vm] * 3 + [sm, vm] + [hbm] * 6,
        out_specs=(vm, vm, vm),
        scratch_shapes=[
            pltpu.VMEM((4 * SH, ENC), BF),
            pltpu.VMEM((4 * SH, ENC), BF),
            pltpu.VMEM((ENC, 512), BF),
            pltpu.VMEM((ENC, 512), BF),
            pltpu.VMEM((1024, 2048), BF),
            pltpu.VMEM((D, 256), BF),
            pltpu.VMEM((4, 8, 384), F32),
            pltpu.VMEM((4, ROWS, ENC), BF),
            pltpu.VMEM((512, 4 * SH), BF),
            pltpu.VMEM((1, 640), F32),
            pltpu.VMEM((512, 640), F32),
            pltpu.VMEM((3, ROWS, ENC), BF),
            pltpu.VMEM((2, ROWS, 640), BF),
            pltpu.VMEM((2, ROWS, ENC), BF),
            pltpu.VMEM((6, 8, 128), F32),
            pltpu.VMEM((5, 3, 8, 128), F32),
            pltpu.VMEM((256, D), BF),
            pltpu.VMEM((256, 256), F32),
            pltpu.VMEM((256, 256), BF),
            pltpu.VMEM((4, 256, 256), BF),
            pltpu.VMEM((8, 128), jnp.int32),
            pltpu.VMEM((4, ROWS, ENC), BF),
            pltpu.VMEM((4, 512, 128), BF),
            pltpu.VMEM((4, 512, 256), BF),
            pltpu.VMEM((256, 512), F32),
            pltpu.VMEM((8, 128), jnp.int32),
            pltpu.VMEM((4, 256, 256), BF),
            pltpu.VMEM((4, 8, 256), F32),
            pltpu.VMEM((4, 256, 256), BF),
            pltpu.VMEM((4, 8, 256), F32),
            pltpu.VMEM((128, 256), F32),
            pltpu.VMEM((256, 1024), BF),
            pltpu.VMEM((256, 1024), F32),
            pltpu.VMEM((3, 64, 2048), BF),
            pltpu.VMEM((2, 64, 1024), BF),
            pltpu.VMEM((2, 64, 2048), BF),
            pltpu.VMEM((64, 2048), BF),
            pltpu.VMEM((4, 16, 2048), BF),
            pltpu.SemaphoreType.DMA((8,)),
            pltpu.SemaphoreType.DMA((NSEM,)),
            pltpu.SemaphoreType.DMA((NSEM,)),
        ],
        compiler_params=pltpu.CompilerParams(
            collective_id=0, has_side_effects=True, vmem_limit_bytes=60 << 20
        ),
        name="block",
    )(
        image, text, ln_gain, ln_bias, b_up, b_down, tile_count, assign, in_gain, q_gain, k_gain,
        attn_gate, amax_hist, w_up.T, w_down, w_key, w_value, w_query, w_out,
    )


def solution(mesh):
    rows = P(("grp", "tp"), None)
    in_specs = (
        rows, rows, P(), P(), P(None, "tp"), P("tp"), P("tp", None), P(), P("grp"), P("grp"),
        P(None, "tp"), P(None, "tp"), P(), P(None, "tp"), P(), P(), P("tp", None), P(), P(),
    )
    return jax.shard_map(local, mesh=mesh, in_specs=in_specs, out_specs=(rows, rows, P()), check_vma=False)
```

time: 404 us -> 169 us (0.42)
  waiting for transfers between devices: 175 us -> 0 us
  blocking collectives: 74.6 us -> 0 us
  Pallas kernels: 93.9 us -> 161 us
  matrix products: 20.5 us -> 0 us
  between operations: 15.3 us -> 1.29 us
  other arithmetic: 9.98 us -> 0 us
  local copies, waits for them, and re-layouts: 11.7 us -> 6.09 us
    reduce_scatter x1 -> x0, waiting for transfers between devices: 91.2 us -> none  [local(): lax.psum_scatter(jnp.dot(attended, w_out, preferred_element_type=jnp.floa...]
    pmax x1 -> x0, blocking collectives: 74.6 us -> none  [local(): cur_text = lax.pmax(cur_text, ('grp', 'tp'))]
    all_gather x2 -> x0, waiting for transfers between devices: 70.2 us -> none  [the longest x1 70.2 us: local(): piece = lax.all_gather(moved, 'tp', axis=0, tiled=True)]
    pallas_call x1, Pallas kernels: 93.9 us -> 161 us  [local(): pl.pallas_call(kernel, out_shape=(jax.ShapeDtypeStruct((16, D), BF), jax....]
    dot_general x6 -> x0, matrix products: 20.5 us -> none  [the longest x1 5.47 us: local(): jnp.dot(lax.all_gather(tnormed_c, 'tp', axis=0, tiled=True), w_query, pre...]
    ppermute x2 -> x0, waiting for transfers between devices: 13.3 us -> none  [passed_along(): lax.ppermute(value, axis, [(i, (i + by) % count) for i in range(count)])]
    broadcast_in_dim x5 -> x0, local copies, waits for them, and re-layouts: 4.65 us -> none  [the longest x1 1.29 us: encoder(): b_down[None, :]]
  transfers between devices with their start and end apart: 5 -> 0, of which waited for: 4 -> 0; matrix products, arithmetic and copies ran while one was open for 4% -> 0% of each run, Pallas kernels for 23% -> 0%
where the time goes in v2:
time: 169 us
  Pallas kernels  161 us (95%)
  local copies, waits for them, and re-layouts  6.09 us (4%)
    pallas_call x1, Pallas kernels, local(): pl.pallas_call(kernel, out_shape=(jax.ShapeDtypeStruct((16, D), BF), jax....  161 us
    unnamed x3, local copies, waits for them, and re-layouts  4.74 us

profile of v2, /device:TPU:40, one launch (start us, length us, event | category | flops | bytes accessed | tf_op | source)
XLA Modules:
  0.0 168.7 jit_solution(6761337935410840707)
XLA Ops:
  1.3 1.4 copy.22.hist
  2.6 161.3 %block.1 = (bf16[16,8192]{1,0:T(8,128)(2,1)}, bf16[128,1280]{1,0:T(8,128)(2,1)}, f32[16,4]{1,0:T(8,128)}) custom-call(bf16[128,1280]{1,0:T(8,128)(2,1)} %image.1, bf16[16,8192]{1,0:T(8,128)(2,1)} %text.1, f32[1280]{0:T(1024)} %lng.1, f32[1280]{0:T(1024)} %lnb.1, f32[320]{0:T(512)} %bup.1, f32[1280]{0:T(1024)} %bdown.1, s32[2]{0:T(128)} %tiles.1, s32[2]{0:T(128)} %assign.1, ...), custom_call_target="tpu_custom_call" | custom-call | tf_op jit(solution)/shard_map/block/pallas_call | solution.py:520
  163.9 1.3 copy.23
  165.3 1.7 copy.27
  167.0 1.7 %copy.28 = bf16[128,1280]{1,0:T(8,128)(2,1)} copy(bf16[128,1280]{1,0:T(8,128)(2,1)} %get-tuple-element.10) | data formatting | bytes 655360

commit v3 on v2

--- a/solution.py
+++ b/solution.py
@@ -14,7 +14,7 @@
 ROWS = 128
 ENC = 1280
 SH = 320
-NSEM = 176
+NSEM = 160
 
 
 class Net:
@@ -162,8 +162,8 @@
     BU[0, 0:1, pl.ds(0, SH)] = bup[...].reshape(1, SH)
     zb = [net.send(BU.at[0], BU.at[(4 - d) % 4], "z", d) for d in (1, 2, 3)]
 
-    limits = jnp.max(hist[...], axis=0, keepdims=True)
-    lim = [limits[:, i : i + 1] for i in range(4)]
+    limits = jnp.max(hist[...], axis=1, keepdims=True)
+    lim = [limits[i : i + 1, :] for i in range(4)]
 
     image_f = image[...].astype(F32)
     centred = image_f - jnp.mean(image_f, axis=-1, keepdims=True)
@@ -326,8 +326,9 @@
     feat_out[...] = FB[0]
 
     cur1 = total_max(HM[...])
-    cur = jnp.where(lane == 0, cur0, 0.0) + jnp.where(lane == 1, cur1, 0.0)
-    cur = cur + jnp.where(lane == 2, cur2, 0.0) + jnp.where(lane == 3, cur3, 0.0)
+    line = lax.broadcasted_iota(jnp.int32, (8, 128), 0)
+    cur = jnp.where(line == 0, cur0, 0.0) + jnp.where(line == 1, cur1, 0.0)
+    cur = cur + jnp.where(line == 2, cur2, 0.0) + jnp.where(line == 3, cur3, 0.0)
     CUR[0] = cur
     stages = (("c", (1,)), ("y", (1, 2, 3)), ("x", (1, 2, 3)), ("z", (1, 2, 3)), ("l", (1,)))
 
@@ -496,8 +497,8 @@
     for d in (2, 1, 3):
         fs[4 - d] = net.send(FS.at[rows_of(((z + d) % 4) * 16, 16)], MX.at[4 - d], "z", d)
     max_take(4, going)
-    amax_out[0:1, :] = CUR[5][0:1, 0:4]
-    amax_out[pl.ds(1, 15), :] = hist[pl.ds(0, 15), :]
+    amax_out[:, 0:1] = CUR[5][0:4, 0:1]
+    amax_out[:, pl.ds(1, 15)] = hist[:, pl.ds(0, 15)]
     strength = jnp.tanh(jnp.full((1, 128), gate[0], F32))[:, 0:1]
     for r in (0, 1, 3, 2):
         cols = rows_of(((z + r) % 4) * 2048, 2048, 128)
@@ -510,6 +511,12 @@
     net.finish()
 
 
+def hand_over(mixed, feat, amax, mixed_out, feat_out, amax_out):
+    mixed_out[...] = mixed[...]
+    feat_out[...] = feat[...]
+    amax_out[...] = amax[...]
+
+
 def local(
     image, text, ln_gain, ln_bias, w_up, b_up, w_down, b_down, tile_count, assign,
     w_key, w_value, in_gain, w_query, q_gain, k_gain, w_out, attn_gate, amax_hist,
@@ -517,12 +524,12 @@
     vm = pl.BlockSpec(memory_space=pltpu.VMEM)
     sm = pl.BlockSpec(memory_space=pltpu.SMEM)
     hbm = pl.BlockSpec(memory_space=pl.ANY)
-    return pl.pallas_call(
+    outs = pl.pallas_call(
         kernel,
         out_shape=(
             jax.ShapeDtypeStruct((16, D), BF),
             jax.ShapeDtypeStruct((ROWS, ENC), BF),
-            jax.ShapeDtypeStruct((16, 4), F32),
+            jax.ShapeDtypeStruct((4, 16), F32),
         ),
         in_specs=[vm] * 6 + [sm] * 2 + [vm] * 3 + [sm, vm] + [hbm] * 6,
         out_specs=(vm, vm, vm),
@@ -575,8 +582,16 @@
         name="block",
     )(
         image, text, ln_gain, ln_bias, b_up, b_down, tile_count, assign, in_gain, q_gain, k_gain,
-        attn_gate, amax_hist, w_up.T, w_down, w_key, w_value, w_query, w_out,
+        attn_gate, amax_hist.T, w_up.T, w_down, w_key, w_value, w_query, w_out,
     )
+    mixed, feat, amax = pl.pallas_call(
+        hand_over,
+        out_shape=[jax.ShapeDtypeStruct(o.shape, o.dtype) for o in outs],
+        in_specs=[vm] * 3,
+        out_specs=[vm] * 3,
+        name="hand_over",
+    )(*outs)
+    return mixed, feat, amax.T
 
 
 def solution(mesh):

time: 169 us -> 164 us (0.970)
  local copies, waits for them, and re-layouts: 6.09 us -> 0 us
    unnamed x3 -> x0, local copies, waits for them, and re-layouts: 4.74 us -> none
    pallas_call x0 -> x1, Pallas kernels: none -> 1.89 us  [local(): pl.pallas_call(hand_over, out_shape=[jax.ShapeDtypeStruct(o.shape, o.dtyp...]
    pallas_call x1, Pallas kernels: 161 us -> 160 us  [local(): pl.pallas_call(kernel, out_shape=(jax.ShapeDtypeStruct((16, D), BF), jax....]
where the time goes in v3:
time: 164 us; the launch traced here: 163 us
  Pallas kernels  161 us (98%)
    pallas_call x1, Pallas kernels, local(): pl.pallas_call(kernel, out_shape=(jax.ShapeDtypeStruct((16, D), BF), jax....  160 us

profile of v3, /device:TPU:40, one launch (start us, length us, event | category | flops | bytes accessed | tf_op | source)
XLA Modules:
  0.0 162.7 jit_solution(15636183089767501780)
XLA Ops:
  1.3 159.6 %block.1 = (bf16[16,8192]{1,0:T(8,128)(2,1)}, bf16[128,1280]{1,0:T(8,128)(2,1)}, f32[4,16]{1,0:T(4,128)}) custom-call(bf16[128,1280]{1,0:T(8,128)(2,1)} %image.1, bf16[16,8192]{1,0:T(8,128)(2,1)} %text.1, f32[1280]{0:T(1024)} %lng.1, f32[1280]{0:T(1024)} %lnb.1, f32[320]{0:T(512)} %bup.1, f32[1280]{0:T(1024)} %bdown.1, s32[2]{0:T(128)} %tiles.1, s32[2]{0:T(128)} %assign.1, ...), custom_call_target="tpu_custom_call" | custom-call | tf_op jit(solution)/shard_map/block/pallas_call | solution.py:527
  160.9 1.9 %hand_over.1 = (bf16[16,8192]{1,0:T(8,128)(2,1)}, bf16[128,1280]{1,0:T(8,128)(2,1)}, f32[4,16]{1,0:T(4,128)}) custom-call(bf16[16,8192]{1,0:T(8,128)(2,1)} %get-tuple-element.9.mixed, bf16[128,1280]{1,0:T(8,128)(2,1)} %get-tuple-element.10.feat, f32[4,16]{1,0:T(4,128)} %get-tuple-element.11.amax), custom_call_target="tpu_custom_call" | custom-call | tf_op jit(solution)/shard_map/hand_over/pallas_call | solution.py:587

commit v4 on v3

--- a/solution.py
+++ b/solution.py
@@ -246,6 +246,12 @@
     gd.swap(1)
     gd.swap(3)
 
+    tz3.wait_recv()
+    tz2a = net.send(T.at[tb(0, zl), tlo], T.at[tb(0, zl), tlo], "z", 1)
+    rings.append(TextRing(zl))
+    tz1.wait_recv()
+    tz2b = net.send(T.at[tb(0, zr), thi], T.at[tb(0, zr), thi], "z", 3)
+    rings.append(TextRing(zr))
     HM[...] = jnp.zeros_like(HM)
 
     def up(pair):
@@ -267,14 +273,12 @@
         lax.fori_loop(0, 2, step, 0)
 
     up(0)
-    tz3.wait_recv()
-    tz2a = net.send(T.at[tb(0, zl), tlo], T.at[tb(0, zl), tlo], "z", 1)
-    rings.append(TextRing(zl))
-    tz1.wait_recv()
-    tz2b = net.send(T.at[tb(0, zr), thi], T.at[tb(0, zr), thi], "z", 3)
-    rings.append(TextRing(zr))
     gd.swap(2)
     gu.ready(2, 3)
+    tz2a.wait_recv()
+    tz2b.wait_recv()
+    zo = (z + 2) % 4
+    rings.append(TextRing(zo))
     up(1)
     own[1].wait()
     gd.ready(1, 2, 3)
@@ -301,10 +305,6 @@
 
     rings[1].relay()
     rings[2].relay()
-    tz2a.wait_recv()
-    tz2b.wait_recv()
-    zo = (z + 2) % 4
-    rings.append(TextRing(zo))
     for part in (gk, gv):
         part.z_got(3)
         part.z_got(1)

time: 164 us -> 163 us (level)
  the two profiles are of different devices: /device:TPU:40 before, /device:TPU:4 now
where the time goes in v4:
time: 163 us
  Pallas kernels  162 us (99%)
    pallas_call x1, Pallas kernels, local(): pl.pallas_call(kernel, out_shape=(jax.ShapeDtypeStruct((16, D), BF), jax....  160 us

profile of v4, /device:TPU:4, one launch (start us, length us, event | category | flops | bytes accessed | tf_op | source)
XLA Modules:
  0.0 163.3 jit_solution(15018951688455209653)
XLA Ops:
  1.3 160.1 %block.1 = (bf16[16,8192]{1,0:T(8,128)(2,1)}, bf16[128,1280]{1,0:T(8,128)(2,1)}, f32[4,16]{1,0:T(4,128)}) custom-call(bf16[128,1280]{1,0:T(8,128)(2,1)} %image.1, bf16[16,8192]{1,0:T(8,128)(2,1)} %text.1, f32[1280]{0:T(1024)} %lng.1, f32[1280]{0:T(1024)} %lnb.1, f32[320]{0:T(512)} %bup.1, f32[1280]{0:T(1024)} %bdown.1, s32[2]{0:T(128)} %tiles.1, s32[2]{0:T(128)} %assign.1, ...), custom_call_target="tpu_custom_call" | custom-call | tf_op jit(solution)/shard_map/block/pallas_call | solution.py:527
  161.4 1.9 %hand_over.1 = (bf16[16,8192]{1,0:T(8,128)(2,1)}, bf16[128,1280]{1,0:T(8,128)(2,1)}, f32[4,16]{1,0:T(4,128)}) custom-call(bf16[16,8192]{1,0:T(8,128)(2,1)} %get-tuple-element.9.mixed, bf16[128,1280]{1,0:T(8,128)(2,1)} %get-tuple-element.10.feat, f32[4,16]{1,0:T(4,128)} %get-tuple-element.11.amax), custom_call_target="tpu_custom_call" | custom-call | tf_op jit(solution)/shard_map/hand_over/pallas_call | solution.py:587
